TPU v7x, 32 devices: a whole 2x2x4 slice. The times are simulated.
32 devices in a mesh: groups: 2 (over y), fsdp: 4 (over z), sub: 2 (over x), pair: 2 (over core).
Axes of the slice: x: 2, y: 2, z: 4, core: 2. Of those that a mesh axis runs over, the one named last changes fastest.
Arguments:
- gradient: float32 [6, 1024, 1024], P('groups', ('fsdp', 'pair'), 'sub'), parts along dimension 0, may hold values from -6 to 6
- owner_table: int32 [6], P('groups'), parts along dimension 0, may hold values from 0 to 3, as said below
- left_basis: bfloat16 [8, 2, 4, 2, 128, 1024], P(('groups', 'fsdp'), None, None, 'pair'), parts along dimension 0, may hold values from -0.1875 to 0.1875
- right_basis: bfloat16 [8, 2, 1024, 1024], P(('groups', 'fsdp'), None, 'sub'), parts along dimension 0, may hold values from -0.1875 to 0.1875
- first_moment: float32 [8, 1024, 2, 1024], P(('groups', 'fsdp'), 'pair', None, 'sub'), parts along dimension 0, may hold values from -3 to 3
- second_moment: float32 [8, 1024, 2, 1024], P(('groups', 'fsdp'), 'pair', None, 'sub'), parts along dimension 0, may hold values from 0.02 to 1
Outputs:
- update: float32 [6, 1024, 1024], P('groups', ('fsdp', 'pair'), 'sub'), parts along dimension 0
- new_first: float32 [8, 1024, 2, 1024], P(('groups', 'fsdp'), 'pair', None, 'sub'), parts along dimension 0
- new_second: float32 [8, 1024, 2, 1024], P(('groups', 'fsdp'), 'pair', None, 'sub'), parts along dimension 0
There are 2 independent parts, one for each index of `groups`. A program takes and returns all parts, laid end to end along the dimension named above; each array names one. Nothing has to cross between parts.
Inputs may be any that keep to these rules, and one draw needn't show every extreme that they name: `owner_table`: no owner is named by more than 2 blocks, and one owner by exactly 2.
All inputs are finite; a program needn't handle non-finite values.
Results may differ from a plain program's by a relative error of at most 0.012.
Values may be sent and summed in bfloat16 or wider, within the bound.
A program may use at most 64 MiB of HBM per device.

v0:
```python
import jax
import jax.numpy as jnp
from jax import lax
from jax.sharding import PartitionSpec as P

STEP = 10


BETA_ONE = 0.95
BETA_TWO = 0.95
EPSILON = 1e-08


def shards(gradient, owner_table, left_basis, right_basis, first_moment, second_moment):
    owners = lax.axis_size("fsdp")
    slot_count = right_basis.shape[1]
    blocks = gradient.shape[0]
    assigned = (owner_table[:, None] == jnp.arange(owners, dtype=jnp.int32)[None, :]).astype(
        jnp.int32
    )
    before = jnp.cumsum(assigned, axis=0) - assigned
    slot_rank = jnp.sum(before * assigned, axis=1)
    placed = assigned[:, None, :] * (
        slot_rank[:, None, None] == jnp.arange(slot_count, dtype=jnp.int32)[None, :, None]
    ).astype(jnp.int32)
    source = jnp.sum(placed * jnp.arange(blocks, dtype=jnp.int32)[:, None, None], axis=0)
    filled = jnp.sum(placed, axis=0)
    outgoing = jnp.where(
        filled[:, :, None, None] > 0,
        gradient[source].astype(jnp.bfloat16),
        jnp.zeros((), jnp.bfloat16),
    )
    arrived = lax.all_to_all(outgoing, "fsdp", split_axis=1, concat_axis=1, tiled=True)
    rows_here = arrived.shape[1] * arrived.shape[2]
    col_share = arrived.shape[3]
    grad_rows = arrived.reshape(slot_count, rows_here, col_share)
    own_index = lax.axis_index("fsdp")
    own_hit = (jnp.arange(owners, dtype=jnp.int32) == own_index).astype(jnp.int32)
    occupied = jnp.sum(filled * own_hit[None, :], axis=1) > 0
    right_rows = right_basis[0]
    order_full = right_rows.shape[2]
    left_rows = left_basis[0, :, :, 0].reshape(slot_count, rows_here, order_full)
    portion = right_rows
    rotated_right = lax.psum_scatter(
        jnp.einsum("skj,sik->jsi", portion, grad_rows, preferred_element_type=jnp.float32).astype(
            jnp.bfloat16
        ),
        "sub",
        scatter_dimension=0,
        tiled=True,
    )
    portion = left_rows
    rotated = lax.psum_scatter(
        jnp.einsum(
            "sir,jsi->rsj", portion, rotated_right, preferred_element_type=jnp.float32
        ).astype(jnp.bfloat16),
        "pair",
        scatter_dimension=0,
        tiled=True,
    ).astype(jnp.float32)
    moment_one = first_moment[0]
    moment_two = second_moment[0]
    corr_one = 1.0 - BETA_ONE**STEP
    corr_two = 1.0 - BETA_TWO**STEP
    next_one = BETA_ONE * moment_one + (1.0 - BETA_ONE) * rotated
    next_two = BETA_TWO * moment_two + (1.0 - BETA_TWO) * rotated * rotated
    keep_slot = occupied[None, :, None]
    new_first = jnp.where(keep_slot, next_one, moment_one)[None]
    new_second = jnp.where(keep_slot, next_two, moment_two)[None]
    normed = (next_one / corr_one / (jnp.sqrt(next_two / corr_two) + EPSILON)).astype(jnp.bfloat16)
    gathered = lax.all_gather(normed, "sub", axis=2, tiled=True)
    back_rot = jnp.einsum("rsj,skj->rsk", gathered, right_rows, preferred_element_type=jnp.float32)
    back_half = back_rot.astype(jnp.bfloat16)
    step_rows = jnp.einsum(
        "sir,rsk->isk",
        left_rows,
        lax.all_gather(back_half, "pair", axis=0, tiled=True),
        preferred_element_type=jnp.float32,
    )
    returned = lax.all_to_all(
        step_rows.reshape(owners, rows_here // owners, slot_count, col_share).astype(jnp.bfloat16),
        "fsdp",
        split_axis=0,
        concat_axis=0,
        tiled=True,
    ).astype(jnp.float32)
    update = returned[owner_table, :, slot_rank]
    return (update, new_first, new_second)


def solution(mesh):
    return jax.shard_map(
        shards,
        mesh=mesh,
        in_specs=(
            P("groups", ("fsdp", "pair"), "sub"),
            P("groups"),
            P(("groups", "fsdp"), None, None, "pair", None, None),
            P(("groups", "fsdp"), None, "sub", None),
            P(("groups", "fsdp"), "pair", None, "sub"),
            P(("groups", "fsdp"), "pair", None, "sub"),
        ),
        out_specs=(
            P("groups", ("fsdp", "pair"), "sub"),
            P(("groups", "fsdp"), "pair", None, "sub"),
            P(("groups", "fsdp"), "pair", None, "sub"),
        ),
        check_vma=False,
    )
```

profile of v0, /device:TPU:0, one launch (start us, length us, event | category | flops | bytes accessed | tf_op | source)
XLA Modules:
  0.0 194.0 jit_solution(2067528776948976607)
XLA Ops:
  7.2 0.9 fusion.22
  8.1 0.8 select_reduce_fusion
  9.0 0.1 fusion.23
  9.0 0.1 multiply_reduce_fusion
  9.1 0.1 reshape.97
  9.2 1.8 gather_fusion
  11.0 0.1 broadcast_select_fusion
  11.2 0.1 copy.36
  11.3 32.0 %all_to_all.10 = bf16[2,4,128,512]{3,2,0,1:T(8,128)(2,1)S(1)} all-to-all(bf16[2,4,128,512]{3,2,0,1:T(8,128)(2,1)S(1)} %copy.36), channel_id=1, replica_groups=mesh['groups'=2,'fsdp'=4,'sub'=2,'pair'=2] {'fsdp'}, dimensions={1} | all-to-all | bytes 2097152 | tf_op jit(solution)/shard_map/all_to_all | solution.py:33
  43.2 0.1 copy.37
  43.4 2.6 %convert_bitcast_fusion.1 = bf16[1024,2,512]{0,2,1:T(8,128)(2,1)} fusion(bf16[2,512,512]{2,1,0:T(8,128)(2,1)S(1)} %bitcast.86, bf16[1,2,512,1024]{3,2,1,0:T(8,128)(2,1)S(1)} %copy-done.2), kind=kOutput, calls=%fused_computation.21 | convolution fusion | flops 1074790400 | bytes 5242880 | tf_op jit(solution)/shard_map/skj,sik->jsi/dot_general | solution.py:45
  46.0 0.0 reduce-scatter.5.cloned.1.call-start
  46.0 31.0 %reduce-scatter.3.cloned.1.call-done = bf16[512,2,512]{0,2,1:T(8,128)(2,1)} async-done(((bf16[1024,2,512]{0,2,1:T(8,128)(2,1)}), bf16[512,2,512]{0,2,1:T(8,128)(2,1)}) %reduce-scatter.3.cloned.1.call-update) | async-done | bytes 1048592 | tf_op jit(solution)/shard_map/reduce_scatter | solution.py:44
  77.0 3.8 %convert_bitcast_fusion = bf16[1024,2,512]{0,2,1:T(8,128)(2,1)} fusion(bf16[512,2,512]{0,2,1:T(8,128)(2,1)} %reduce-scatter.3.cloned.1.call-done, bf16[2,512,1024]{2,1,0:T(8,128)(2,1)S(1)} %bitcast.83), kind=kOutput, calls=%fused_computation.20 | convolution fusion | flops 1074790400 | bytes 5242880 | tf_op jit(solution)/shard_map/sir,jsi->rsj/dot_general | solution.py:54
  80.9 0.0 all-gather.3.cloned.1.call-start
  81.0 4.1 %copy.35 = f32[1,512,2,512]{1,3,2,0:T(8,128)} copy(f32[1,512,2,512]{3,2,1,0:T(2,128)} %param.10) | data formatting | bytes 4194304 | tf_op args[4]
  85.1 4.1 %copy.39 = f32[1,512,2,512]{1,3,2,0:T(8,128)} copy(f32[1,512,2,512]{3,2,1,0:T(2,128)} %param.11) | data formatting | bytes 4194304 | tf_op args[5]
  89.2 0.1 multiply_reduce_fusion.1
  89.4 1.3 reduce-scatter.5.cloned.1.call-done
  90.7 7.0 %fusion.5 = (f32[1,512,2,512]{1,3,2,0:T(8,128)}, bf16[512,2,512]{0,2,1:T(8,128)(2,1)}, f32[1,512,2,512]{1,3,2,0:T(8,128)}) fusion(bf16[512,2,512]{0,2,1:T(8,128)(2,1)} %reduce-scatter.5.cloned.1.call-done, f32[1,512,2,512]{1,3,2,0:T(8,128)} %copy.39, pred[2]{0:T(512)(128)(4,1)S(1)} %broadcast_compare_fusion.1, f32[1,512,2,512]{1,3,2,0:T(8,128)} %copy.35), kind=kLoop, calls=%fused_computation.11 | loop fusion | flops 7340032 | bytes 10485762 | tf_op jit(solution)/shard_map/broadcast_in_dim | solution.py:69
  97.7 0.0 all-gather.5.cloned.1.call-start
  97.8 34.4 %all-gather.3.cloned.1.call-done = bf16[512,2,1024]{0,2,1:T(8,128)(2,1)} async-done(((bf16[512,2,512]{0,2,1:T(8,128)(2,1)}), bf16[512,2,1024]{0,2,1:T(8,128)(2,1)}) %all-gather.3.cloned.1.call-update) | async-done | bytes 2097168 | tf_op jit(solution)/shard_map/all_gather | solution.py:71
  132.2 4.8 %fusion.18 = bf16[512,2,512]{2,0,1:T(8,128)(2,1)} fusion(bf16[512,2,1024]{0,2,1:T(8,128)(2,1)} %all-gather.3.cloned.1.call-done, bf16[1,2,512,1024]{3,2,1,0:T(8,128)(2,1)} %param.9), kind=kOutput, calls=%fused_computation.25 | convolution fusion | flops 1074266112 | bytes 5242880 | tf_op jit(solution)/shard_map/rsj,skj->rsk/dot_general | solution.py:72
  137.0 10.7 %all-gather.5.cloned.1.call-done = bf16[1024,2,512]{2,0,1:T(8,128)(2,1)} async-done(((bf16[512,2,512]{2,0,1:T(8,128)(2,1)}), bf16[1024,2,512]{2,0,1:T(8,128)(2,1)}) %all-gather.5.cloned.1.call-update) | async-done | bytes 2097168 | tf_op jit(solution)/shard_map/all_gather | solution.py:77
  147.7 2.8 %convolution_convert_fusion = bf16[2,512,512]{1,2,0:T(8,128)(2,1)S(1)} fusion(bf16[2,512,1024]{2,1,0:T(8,128)(2,1)S(1)} %bitcast.84, bf16[1024,2,512]{2,0,1:T(8,128)(2,1)} %all-gather.5.cloned.1.call-done), kind=kOutput, calls=%fused_computation.24 | convolution fusion | flops 1074266112 | bytes 5242880 | tf_op jit(solution)/shard_map/sir,rsk->isk/dot_general | solution.py:74
  150.6 1.1 copy.41
  151.7 4.9 %all-to-all-start.1 = ((bf16[4,128,2,512]{3,1,2,0:T(8,128)(2,1)}), bf16[4,128,2,512]{3,1,2,0:T(8,128)(2,1)S(1)}, u32[]{:S(2)}, u32[]{:S(2)}) async-start(bf16[4,128,2,512]{3,1,2,0:T(8,128)(2,1)} %copy.41), calls=%async_computation.3 | async-start | bytes 2097152 | tf_op jit(solution)/shard_map/all_to_all | solution.py:80
  156.5 4.1 %copy.43 = f32[1,512,2,512]{3,2,1,0:T(2,128)} copy(f32[1,512,2,512]{1,3,2,0:T(8,128)} %get-tuple-element.20) | data formatting | bytes 4194304
  160.7 4.1 %copy.42 = f32[1,512,2,512]{3,2,1,0:T(2,128)} copy(f32[1,512,2,512]{1,3,2,0:T(8,128)} %get-tuple-element.22) | data formatting | bytes 4194304
  164.8 18.0 %all-to-all-done.1 = bf16[4,128,2,512]{3,1,2,0:T(8,128)(2,1)S(1)} async-done(((bf16[4,128,2,512]{3,1,2,0:T(8,128)(2,1)}), bf16[4,128,2,512]{3,1,2,0:T(8,128)(2,1)S(1)}, u32[]{:S(2)}, u32[]{:S(2)}) %all-to-all-start.1) | async-done | bytes 1048608 | tf_op jit(solution)/shard_map/all_to_all | solution.py:80
  182.7 1.6 convert_element_type.75
  184.4 3.1 %gather_fusion.1 = f32[3,128,512]{2,1,0:T(8,128)} fusion(f32[4,128,2,512]{3,1,2,0:T(8,128)} %convert_element_type.75, s32[3]{0:T(128)S(1)} %fusion.30), kind=kCustom, calls=%fused_computation.1 | custom fusion | bytes 1572888 | tf_op jit(solution)/shard_map/gather | solution.py:87
  (18 shorter events, 0.2 us)
Async XLA Ops:
  7.2 69.9 %copy-start = (bf16[1,2,4,1,128,1024]{5,4,3,2,1,0:T(8,128)(2,1)S(1)}, bf16[1,2,4,1,128,1024]{5,4,3,2,1,0:T(8,128)(2,1)}, u32[]{:S(2)}) copy-start(bf16[1,2,4,1,128,1024]{5,4,3,2,1,0:T(8,128)(2,1)} %param.8) | copy-start | bytes 6291460
  7.2 69.9 %reduce-scatter.3.cloned.1.call-start = ((), (), s32[]{:S(2)}) async-start(), calls=%async_computation.4 | async-start | bytes 3145728 | tf_op jit(solution)/shard_map/reduce_scatter | solution.py:44
  11.2 32.1 %copy-start.2 = (bf16[1,2,512,1024]{3,2,1,0:T(8,128)(2,1)S(1)}, bf16[1,2,512,1024]{3,2,1,0:T(8,128)(2,1)}, u32[]{:S(2)}) copy-start(bf16[1,2,512,1024]{3,2,1,0:T(8,128)(2,1)} %param.9) | copy-start | bytes 6291460
  46.0 44.7 %reduce-scatter.5.cloned.1.call-start = ((), (), s32[]{:S(2)}) async-start(), calls=%async_computation.5 | async-start | bytes 3145728 | tf_op jit(solution)/shard_map/reduce_scatter | solution.py:53
  80.9 51.3 %all-gather.3.cloned.1.call-start = ((), (), s32[]{:S(2)}) async-start(), calls=%async_computation.6 | async-start | bytes 3145728 | tf_op jit(solution)/shard_map/all_gather | solution.py:71
  97.7 50.0 %all-gather.5.cloned.1.call-start = ((), (), s32[]{:S(2)}) async-start(), calls=%async_computation.7 | async-start | bytes 3145728 | tf_op jit(solution)/shard_map/all_gather | solution.py:77
  150.6 6.0 %copy-start.1 = (s32[3]{0:T(128)S(1)}, s32[3]{0:T(128)}, u32[]{:S(2)}) copy-start(s32[3]{0:T(128)} %param.7) | copy-start | bytes 40
  151.7 31.0 %all-to-all-start.1 = ((bf16[4,128,2,512]{3,1,2,0:T(8,128)(2,1)}), bf16[4,128,2,512]{3,1,2,0:T(8,128)(2,1)S(1)}, u32[]{:S(2)}, u32[]{:S(2)}) async-start(bf16[4,128,2,512]{3,1,2,0:T(8,128)(2,1)} %copy.41), calls=%async_computation.3 | async-start | bytes 2097152 | tf_op jit(solution)/shard_map/all_to_all | solution.py:80
Sparse Core Ops, SparseCore 0:
  46.1 30.9 reduce-scatter.2
  81.0 9.5 reduce-scatter.4
  97.8 34.2 all-gather.2
  137.1 10.5 all-gather.4
where the time goes:
time: 195 us; the launch traced here: 194 us
  waiting for transfers between devices  95.5 us (49%)
  blocking collectives  32 us (16%)
  local copies, waits for them, and re-layouts  22.7 us (12%)
  matrix products  14 us (7%)
  between operations  13.9 us (7%)
  other arithmetic  10.9 us (6%)
  starting transfers between devices  5.02 us (3%)
    all_gather x1, waiting for transfers between devices, shards(): gathered = lax.all_gather(normed, 'sub', axis=2, tiled=True)  34.4 us
    all_to_all x1, blocking collectives, shards(): lax.all_to_all(outgoing, 'fsdp', split_axis=1, concat_axis=1, tiled=True)  32 us
    reduce_scatter x1, waiting for transfers between devices, shards(): lax.psum_scatter(jnp.einsum('skj,sik->jsi', portion, grad_rows, preferred...  31 us
    all_to_all x1, waiting for transfers between devices, shards(): lax.all_to_all(step_rows.reshape(owners, rows_here // owners, slot_count,...  18 us
    unnamed x10, local copies, waits for them, and re-layouts  16.5 us
    all_gather x1, waiting for transfers between devices, shards(): lax.all_gather(back_half, 'pair', axis=0, tiled=True)  10.7 us
    broadcast_in_dim x1, other arithmetic, shards(): new_second = jnp.where(keep_slot, next_two, moment_two)[None]  7.03 us
    all_to_all x1, starting transfers between devices, shards(): lax.all_to_all(step_rows.reshape(owners, rows_here // owners, slot_count,...  4.86 us
  transfers between devices with their start and end apart: 5, of which 5 were waited for; matrix products, arithmetic and copies ran while one was open for 9% of the time, Pallas kernels for 0%

commit v1 on v0

v1 whole, which is shorter than its diff:
```python
import functools

import jax
import jax.numpy as jnp
from jax import lax
from jax.experimental import pallas as pl
from jax.experimental.pallas import tpu as pltpu
from jax.sharding import PartitionSpec as P

STEP = 10


BETA_ONE = 0.95
BETA_TWO = 0.95
EPSILON = 1e-08

MESH = pl.DeviceIdType.MESH
BF = jnp.bfloat16
F32 = jnp.float32


def send(src, dst, send_sem, recv_sem, where):
    return pltpu.make_async_remote_copy(
        src_ref=src,
        dst_ref=dst,
        send_sem=send_sem,
        recv_sem=recv_sem,
        device_id=where,
        device_id_type=MESH,
    )


def kernel(
    owners,
    subs,
    table,
    grad,
    left_hbm,
    right_hbm,
    one_hbm,
    two_hbm,
    update,
    one_out,
    two_out,
    left,
    left_t,
    right,
    one,
    two,
    one_new,
    two_new,
    grad_send,
    grad_recv,
    part_send,
    part_recv,
    part_own,
    rot_send,
    rot_recv,
    rot_own,
    normed,
    back,
    step_send,
    step_recv,
    load_sem,
    store_sem,
    gs_sem,
    gr_sem,
    ps_sem,
    pr_sem,
    rs_sem,
    rr_sem,
    ns_sem,
    nr_sem,
    bs_sem,
    br_sem,
    us_sem,
    ur_sem,
):
    blocks, shard, share = grad.shape
    slots, half, order = left.shape
    tile = min(256, share)
    z = lax.axis_index("fsdp")
    x = lax.axis_index("sub")
    c = lax.axis_index("pair")
    z_peers = [lax.rem(z + d, owners) for d in range(1, owners)]
    x_peers = [lax.rem(x + d, subs) for d in range(1, subs)]

    loads = [
        pltpu.make_async_copy(src, dst, load_sem.at[n])
        for n, (src, dst) in enumerate(
            ((right_hbm, right), (left_hbm, left), (one_hbm, one), (two_hbm, two))
        )
    ]
    for load in loads:
        load.start()

    barrier = pltpu.get_barrier_semaphore()
    for o in z_peers:
        pl.semaphore_signal(barrier, inc=1, device_id={"fsdp": o}, device_id_type=MESH)
    for s in x_peers:
        pl.semaphore_signal(barrier, inc=1, device_id={"sub": s}, device_id_type=MESH)
    pl.semaphore_signal(barrier, inc=1, device_id={"pair": 1 - c}, device_id_type=MESH)

    owner = [table[b] for b in range(blocks)]
    rank = []
    for b in range(blocks):
        r = jnp.int32(0)
        for e in range(b):
            r = r + jnp.where(owner[e] == owner[b], 1, 0)
        rank.append(r)

    def source(o, k):
        n = jnp.int32(0)
        for b in range(blocks):
            n = n + jnp.where((owner[b] == o) & (rank[b] == k), b, 0)
        return n

    count = jnp.int32(0)
    for b in range(blocks):
        count = count + jnp.where(owner[b] == z, 1, 0)

    pending = []
    for k in range(slots):
        for d, o in enumerate(z_peers):
            grad_send[k, d] = grad[source(o, k)].astype(BF)
            if k == 0 and d == 0:
                pl.semaphore_wait(barrier, len(z_peers) + len(x_peers) + 1)
            copy = send(
                grad_send.at[k, d],
                grad_recv.at[k, z],
                gs_sem.at[k, d],
                gr_sem.at[k, z],
                {"fsdp": o},
            )
            copy.start()
            pending.append(copy)
        grad_recv[k, z] = grad[source(z, k)].astype(BF)

    loads[0].wait()
    loads[1].wait()
    for k in range(slots):
        for n in range(0, half, tile):
            left_t[k, :, n : n + tile] = left[k, n : n + tile, :].T

    def wait_from(buffer, sems, k, peers, axis):
        for p in peers:
            send(buffer.at[k, p], buffer.at[k, p], sems.at[k, p], sems.at[k, p], {axis: p}).wait_recv()

    def columns(s, n):
        return pl.ds(pl.multiple_of(s * share + n, tile), tile)

    def rotate_right(k):
        wait_from(grad_recv, gr_sem, k, z_peers, "fsdp")
        g = grad_recv[k].reshape(half, share)
        for d, s in enumerate(x_peers):
            for n in range(0, share, tile):
                part_send[k, d, :, n : n + tile] = jnp.dot(
                    g, right[k, :, columns(s, n)], preferred_element_type=F32
                ).astype(BF)
            copy = send(
                part_send.at[k, d],
                part_recv.at[k, x],
                ps_sem.at[k, d],
                pr_sem.at[k, x],
                {"sub": s},
            )
            copy.start()
            pending.append(copy)
        for n in range(0, share, tile):
            part_own[k, :, n : n + tile] = jnp.dot(
                g, right[k, :, columns(x, n)], preferred_element_type=F32
            ).astype(BF)

    def rotate_left(k):
        wait_from(part_recv, pr_sem, k, x_peers, "sub")
        for n in range(0, share, tile):
            cols = slice(n, n + tile)
            total = part_own[k, :, cols].astype(F32)
            for s in x_peers:
                total = total + part_recv[k, s, :, cols].astype(F32)
            part_own[k, :, cols] = total.astype(BF)
        other = pl.ds(pl.multiple_of((1 - c) * half, half), half)
        mine = pl.ds(pl.multiple_of(c * half, half), half)
        for n in range(0, share, tile):
            cols = slice(n, n + tile)
            rot_send[k, :, cols] = jnp.dot(
                left_t[k, other, :], part_own[k, :, cols], preferred_element_type=F32
            ).astype(BF)
        copy = send(rot_send.at[k], rot_recv.at[k], rs_sem.at[k], rr_sem.at[k], {"pair": 1 - c})
        copy.start()
        pending.append(copy)
        for n in range(0, share, tile):
            cols = slice(n, n + tile)
            rot_own[:, cols] = jnp.dot(
                left_t[k, mine, :], part_own[k, :, cols], preferred_element_type=F32
            )
        copy.wait_recv()

    corr_one = 1.0 - BETA_ONE**STEP
    corr_two = 1.0 - BETA_TWO**STEP

    def moments(k):
        used = count > k
        rows = 32

        @pl.loop(0, half // rows)
        def _(i):
            at = pl.ds(pl.multiple_of(i * rows, rows), rows)
            r = rot_own[at, :] + rot_recv[k, at, :].astype(F32)
            m_old = one[at, k, :]
            v_old = two[at, k, :]
            m = BETA_ONE * m_old + (1.0 - BETA_ONE) * r
            v = BETA_TWO * v_old + (1.0 - BETA_TWO) * r * r
            one_new[at, k, :] = jnp.where(used, m, m_old)
            two_new[at, k, :] = jnp.where(used, v, v_old)
            normed[k, x, at, :] = (
                m / corr_one / (jnp.sqrt(v / corr_two) + EPSILON)
            ).astype(BF)

        for d, s in enumerate(x_peers):
            copy = send(
                normed.at[k, x],
                normed.at[k, x],
                ns_sem.at[k, d],
                nr_sem.at[k, x],
                {"sub": s},
            )
            copy.start()
            pending.append(copy)

    def back_rotate(k):
        wait_from(normed, nr_sem, k, x_peers, "sub")
        for n in range(0, share, tile):
            total = jnp.zeros((half, tile), F32)
            for s in range(subs):
                total = total + lax.dot_general(
                    normed[k, s],
                    right[k, n : n + tile, s * share : (s + 1) * share],
                    (((1,), (1,)), ((), ())),
                    preferred_element_type=F32,
                )
            back[k, c, :, n : n + tile] = total.astype(BF)
        copy = send(back.at[k, c], back.at[k, c], bs_sem.at[k], br_sem.at[k], {"pair": 1 - c})
        copy.start()
        pending.append(copy)
        send(
            back.at[k, 1 - c], back.at[k, 1 - c], bs_sem.at[k], br_sem.at[k], {"pair": 1 - c}
        ).wait_recv()
        b = back[k].reshape(order, share)
        for n in range(0, share, tile):
            rows = jnp.dot(left[k], b[:, n : n + tile], preferred_element_type=F32).astype(BF)
            step_send[k, :, :, n : n + tile] = rows.reshape(owners, shard, tile)
        for d, o in enumerate(z_peers):
            copy = send(
                step_send.at[k, o],
                step_recv.at[k, z],
                us_sem.at[k, d],
                ur_sem.at[k, z],
                {"fsdp": o},
            )
            copy.start()
            pending.append(copy)
        step_recv[k, z] = step_send[k, z]

    rotate_right(0)
    rotate_right(1)
    rotate_left(0)
    loads[2].wait()
    loads[3].wait()
    moments(0)
    rotate_left(1)
    moments(1)
    stores = [
        pltpu.make_async_copy(one_new, one_out, store_sem.at[0]),
        pltpu.make_async_copy(two_new, two_out, store_sem.at[1]),
    ]
    for store in stores:
        store.start()
    back_rotate(0)
    back_rotate(1)
    for k in range(slots):
        wait_from(step_recv, ur_sem, k, z_peers, "fsdp")
    for b in range(blocks):
        update[b] = step_recv[jnp.minimum(rank[b], slots - 1), owner[b]].astype(F32)
    for copy in pending:
        copy.wait_send()
    for store in stores:
        store.wait()


def shards(
    owners, subs, gradient, owner_table, left_basis, right_basis, first_moment, second_moment
):
    slots, order = right_basis.shape[1], right_basis.shape[3]
    blocks, shard, share = gradient.shape
    half = owners * shard
    left_rows = left_basis.reshape(slots, half, order)
    right_rows = right_basis.reshape(slots, share, order)
    one = first_moment.reshape(half, slots, share)
    two = second_moment.reshape(half, slots, share)
    dma = pltpu.SemaphoreType.DMA
    whole = pl.BlockSpec(memory_space=pl.ANY)
    vmem = pl.BlockSpec(memory_space=pltpu.VMEM)
    moment = jax.ShapeDtypeStruct((half, slots, share), F32)
    update, new_one, new_two = pl.pallas_call(
        functools.partial(kernel, owners, subs),
        out_shape=(jax.ShapeDtypeStruct((blocks, shard, share), F32), moment, moment),
        in_specs=[pl.BlockSpec(memory_space=pltpu.SMEM), vmem, whole, whole, whole, whole],
        out_specs=(vmem, whole, whole),
        scratch_shapes=[
            pltpu.VMEM((slots, half, order), BF),
            pltpu.VMEM((slots, order, half), BF),
            pltpu.VMEM((slots, share, order), BF),
            pltpu.VMEM((half, slots, share), F32),
            pltpu.VMEM((half, slots, share), F32),
            pltpu.VMEM((half, slots, share), F32),
            pltpu.VMEM((half, slots, share), F32),
            pltpu.VMEM((slots, owners - 1, shard, share), BF),
            pltpu.VMEM((slots, owners, shard, share), BF),
            pltpu.VMEM((slots, subs - 1, half, share), BF),
            pltpu.VMEM((slots, subs, half, share), BF),
            pltpu.VMEM((slots, half, share), BF),
            pltpu.VMEM((slots, half, share), BF),
            pltpu.VMEM((slots, half, share), BF),
            pltpu.VMEM((half, share), F32),
            pltpu.VMEM((slots, subs, half, share), BF),
            pltpu.VMEM((slots, 2, half, share), BF),
            pltpu.VMEM((slots, owners, shard, share), BF),
            pltpu.VMEM((slots, owners, shard, share), BF),
            dma((4,)),
            dma((2,)),
            dma((slots, owners)),
            dma((slots, owners)),
            dma((slots, subs)),
            dma((slots, subs)),
            dma((slots,)),
            dma((slots,)),
            dma((slots, subs)),
            dma((slots, subs)),
            dma((slots,)),
            dma((slots,)),
            dma((slots, owners)),
            dma((slots, owners)),
        ],
        compiler_params=pltpu.CompilerParams(
            collective_id=0, has_side_effects=True, vmem_limit_bytes=48 * 2**20
        ),
        cost_estimate=pl.CostEstimate(
            flops=10 * slots * half * order * share,
            bytes_accessed=20 * slots * half * share,
            transcendentals=slots * half * share,
        ),
    )(owner_table, gradient, left_rows, right_rows, one, two)
    return (update, new_one[None], new_two[None])


def solution(mesh):
    return jax.shard_map(
        functools.partial(shards, mesh.shape["fsdp"], mesh.shape["sub"]),
        mesh=mesh,
        in_specs=(
            P("groups", ("fsdp", "pair"), "sub"),
            P("groups"),
            P(("groups", "fsdp"), None, None, "pair", None, None),
            P(("groups", "fsdp"), None, "sub", None),
            P(("groups", "fsdp"), "pair", None, "sub"),
            P(("groups", "fsdp"), "pair", None, "sub"),
        ),
        out_specs=(
            P("groups", ("fsdp", "pair"), "sub"),
            P(("groups", "fsdp"), "pair", None, "sub"),
            P(("groups", "fsdp"), "pair", None, "sub"),
        ),
        check_vma=False,
    )
```

time: 195 us -> 87.1 us (0.45)
  the two profiles are of different devices: /device:TPU:0 before, /device:TPU:29 now
where the time goes in v1:
time: 87.1 us; the launch traced here: 87 us
  Pallas kernels  81 us (93%)
  local copies, waits for them, and re-layouts  5.3 us (6%)
    pallas_call x1, Pallas kernels, shards(): pl.pallas_call(functools.partial(kernel, owners, subs), out_shape=(jax.Sh...  81 us
    unnamed x7, local copies, waits for them, and re-layouts  5.3 us

profile of v1, /device:TPU:29, one launch (start us, length us, event | category | flops | bytes accessed | tf_op | source)
XLA Modules:
  0.0 87.0 jit_solution(9114029870841928308)
XLA Ops:
  0.6 0.0 copy-start
  0.6 1.1 %copy-done = f32[3,128,512]{2,1,0:T(8,128)S(1)} copy-done((f32[3,128,512]{2,1,0:T(8,128)S(1)}, f32[3,128,512]{2,1,0:T(8,128)}, u32[]{:S(2)}) %copy-start) | copy-done | bytes 786456
  1.8 0.0 copy-start.1
  1.8 0.7 copy-done.1
  2.4 81.0 %shard_map.85 = (f32[3,128,512]{2,1,0:T(8,128)S(1)}, f32[512,2,512]{2,1,0:T(2,128)S(1)}, f32[512,2,512]{2,1,0:T(2,128)S(1)}) custom-call(s32[3]{0:T(128)S(1)} %copy-done.1, f32[3,128,512]{2,1,0:T(8,128)S(1)} %copy-done, bf16[2,512,1024]{2,1,0:T(8,128)(2,1)} %bitcast.8, bf16[2,512,1024]{2,1,0:T(8,128)(2,1)} %bitcast.9, f32[512,2,512]{2,1,0:T(2,128)} %bitcast.10, ...), custom_call_target="tpu_custom_call" | custom-call | flops 5368709120 | bytes 10485760 | tf_op jit(solution)/shard_map/pallas_call | solution.py:305
  83.5 0.9 %copy.12 = f32[3,128,512]{2,1,0:T(8,128)} copy(f32[3,128,512]{2,1,0:T(8,128)S(1)} %get-tuple-element.12) | data formatting | bytes 1572864
  84.3 1.3 %copy.13 = f32[1,512,2,512]{3,2,1,0:T(2,128)} copy(f32[1,512,2,512]{3,2,1,0:T(2,128)S(1)} %bitcast.7) | data formatting | bytes 4194304
  85.7 1.3 %copy.14 = f32[1,512,2,512]{3,2,1,0:T(2,128)} copy(f32[1,512,2,512]{3,2,1,0:T(2,128)S(1)} %bitcast.6) | data formatting | bytes 4194304
Async XLA Ops:
  0.6 1.1 %copy-start = (f32[3,128,512]{2,1,0:T(8,128)S(1)}, f32[3,128,512]{2,1,0:T(8,128)}, u32[]{:S(2)}) copy-start(f32[3,128,512]{2,1,0:T(8,128)} %grad.1) | copy-start | bytes 2359300
  1.8 0.7 copy-start.1

commit v2 on v1

v2 whole, which is shorter than its diff:
```python
import functools

import jax
import jax.numpy as jnp
from jax import lax
from jax.experimental import pallas as pl
from jax.experimental.pallas import tpu as pltpu
from jax.sharding import PartitionSpec as P

STEP = 10


BETA_ONE = 0.95
BETA_TWO = 0.95
EPSILON = 1e-08

MESH = pl.DeviceIdType.MESH
BF = jnp.bfloat16
F32 = jnp.float32


def send(src, dst, send_sem, recv_sem, where):
    return pltpu.make_async_remote_copy(
        src_ref=src,
        dst_ref=dst,
        send_sem=send_sem,
        recv_sem=recv_sem,
        device_id=where,
        device_id_type=MESH,
    )


def kernel(
    owners,
    subs,
    table,
    grad,
    left_hbm,
    right_hbm,
    one_hbm,
    two_hbm,
    update,
    one_out,
    two_out,
    left,
    left_t,
    right,
    one,
    two,
    one_new,
    two_new,
    grad_own,
    grad_far,
    grad_send,
    grad_recv,
    late_send,
    late_recv,
    far_send,
    far,
    part_send,
    part_recv,
    part_own,
    rot_send,
    rot_recv,
    rot_own,
    normed,
    back_sum,
    back,
    step_send,
    step_recv,
    load_sem,
    store_sem,
    gs_sem,
    gr_sem,
    as_sem,
    ar_sem,
    ls_sem,
    lr_sem,
    fs_sem,
    fr_sem,
    hs_sem,
    hr_sem,
    ps_sem,
    pr_sem,
    rs_sem,
    rr_sem,
    ns_sem,
    nr_sem,
    bs_sem,
    br_sem,
    us_sem,
    ur_sem,
):
    blocks, shard, share = grad.shape
    slots, half, order = left.shape
    tile = min(256, share)
    z = lax.axis_index("fsdp")
    x = lax.axis_index("sub")
    c = lax.axis_index("pair")
    z_peers = [lax.rem(z + d, owners) for d in range(1, owners)]
    x_peers = [lax.rem(x + d, subs) for d in range(1, subs)]

    loads = [
        pltpu.make_async_copy(src, dst, load_sem.at[n])
        for n, (src, dst) in enumerate(
            ((right_hbm, right), (left_hbm, left), (one_hbm, one), (two_hbm, two))
        )
    ]
    for load in loads:
        load.start()

    barrier = pltpu.get_barrier_semaphore()
    for o in z_peers:
        pl.semaphore_signal(barrier, inc=1, device_id={"fsdp": o}, device_id_type=MESH)
    for s in x_peers:
        pl.semaphore_signal(barrier, inc=1, device_id={"sub": s}, device_id_type=MESH)
    pl.semaphore_signal(barrier, inc=1, device_id={"pair": 1 - c}, device_id_type=MESH)

    owner = [table[b] for b in range(blocks)]
    rank = []
    for b in range(blocks):
        r = jnp.int32(0)
        for e in range(b):
            r = r + jnp.where(owner[e] == owner[b], 1, 0)
        rank.append(r)

    def source(o, k):
        n = jnp.int32(0)
        for b in range(blocks):
            n = n + jnp.where((owner[b] == o) & (rank[b] == k), b, 0)
        return n

    count = jnp.int32(0)
    for b in range(blocks):
        count = count + jnp.where(owner[b] == z, 1, 0)

    last = slots - 1
    chunks = share // tile
    part = share // 2
    other = pl.ds(pl.multiple_of((1 - c) * half, half), half)
    mine = pl.ds(pl.multiple_of(c * half, half), half)
    pending = []

    def go(src, dst, send_sem, recv_sem, where):
        copy = send(src, dst, send_sem, recv_sem, where)
        copy.start()
        pending.append(copy)
        return copy

    def arrive(ref, sem, where):
        send(ref, ref, sem, sem, where).wait_recv()

    grad_own[...] = grad[...].astype(BF)
    pl.semaphore_wait(barrier, len(z_peers) + len(x_peers) + 1)
    early = []
    for k in range(last):
        for d, o in enumerate(z_peers):
            grad_send[k, d] = grad_own[source(o, k)]
            copy = send(
                grad_send.at[k, d], grad_recv.at[k, z], gs_sem.at[k, d], gr_sem.at[k, z], {"fsdp": o}
            )
            copy.start()
            early.append(copy)
        grad_recv[k, z] = grad_own[source(z, k)]
    for d, s in enumerate(x_peers):
        go(grad_own, grad_far.at[x], as_sem.at[d], ar_sem.at[x], {"sub": s})

    def columns(s, n):
        return pl.ds(pl.multiple_of(s * share + n, tile), tile)

    def columns_of(s):
        return pl.ds(pl.multiple_of(s * share, share), share)

    loads[0].wait()
    for d, s in enumerate(x_peers):
        far_send[d] = right[last, pl.ds(pl.multiple_of(c * part, part), part), columns_of(s)]
        go(far_send.at[d], far.at[x, c], fs_sem.at[d], fr_sem.at[x], {"sub": s})

    loads[1].wait()
    for k in range(slots):
        for n in range(0, half, tile):
            left_t[k, :, n : n + tile] = left[k, n : n + tile, :].T

    for copy in early:
        copy.wait_send()
    for n, s in enumerate([x] + x_peers):
        if n == 1:
            for p in x_peers:
                arrive(grad_far.at[p], ar_sem.at[p], {"sub": p})
        rows = (lambda i: grad_far[s, i]) if n else (lambda i: grad_own[i])
        for d, o in enumerate(z_peers):
            late_send[n, d] = rows(source(o, last))
            go(
                late_send.at[n, d],
                late_recv.at[n, z],
                ls_sem.at[n, d],
                lr_sem.at[n, z],
                {"fsdp": o},
            )
        late_recv[n, z] = rows(source(z, last))
    for d, s in enumerate(x_peers):
        arrive(far.at[s, c], fr_sem.at[s], {"sub": s})
        go(far.at[s, c], far.at[s, c], hs_sem.at[d], hr_sem.at[d], {"pair": 1 - c})

    def rotate_right(k):
        for p in z_peers:
            arrive(grad_recv.at[k, p], gr_sem.at[k, p], {"fsdp": p})
        g = grad_recv[k].reshape(half, share)
        for ch in range(chunks):
            for d, s in enumerate(x_peers):
                part_send[k, d, ch] = jnp.dot(
                    g, right[k, :, columns(s, ch * tile)], preferred_element_type=F32
                ).astype(BF)
                go(
                    part_send.at[k, d, ch],
                    part_recv.at[k, x, ch],
                    ps_sem.at[k, d, ch],
                    pr_sem.at[k, x, ch],
                    {"sub": s},
                )
        for ch in range(chunks):
            part_own[k, ch] = jnp.dot(
                g, right[k, :, columns(x, ch * tile)], preferred_element_type=F32
            ).astype(BF)

    def collect(k, ch):
        total = part_own[k, ch].astype(F32)
        for s in x_peers:
            arrive(part_recv.at[k, s, ch], pr_sem.at[k, s, ch], {"sub": s})
            total = total + part_recv[k, s, ch].astype(F32)
        part_own[k, ch] = total.astype(BF)

    def rotate_right_last():
        for n in range(subs):
            for p in z_peers:
                arrive(late_recv.at[n, p], lr_sem.at[n, p], {"fsdp": p})
        for d, s in enumerate(x_peers):
            arrive(far.at[s, 1 - c], hr_sem.at[d], {"pair": 1 - c})
        for ch in range(chunks):
            total = jnp.dot(
                late_recv[0].reshape(half, share),
                right[last, :, columns(x, ch * tile)],
                preferred_element_type=F32,
            )
            for n, s in enumerate(x_peers):
                total = total + jnp.dot(
                    late_recv[n + 1].reshape(half, share),
                    far[s].reshape(share, share)[:, ch * tile : (ch + 1) * tile],
                    preferred_element_type=F32,
                )
            part_own[last, ch] = total.astype(BF)

    def rotate_left(k, ch):
        rot_send[k, ch] = jnp.dot(
            left_t[k, other, :], part_own[k, ch], preferred_element_type=F32
        ).astype(BF)
        go(
            rot_send.at[k, ch],
            rot_recv.at[k, ch],
            rs_sem.at[k, ch],
            rr_sem.at[k, ch],
            {"pair": 1 - c},
        )
        rot_own[...] = jnp.dot(left_t[k, mine, :], part_own[k, ch], preferred_element_type=F32)
        arrive(rot_recv.at[k, ch], rr_sem.at[k, ch], {"pair": 1 - c})

    corr_one = 1.0 - BETA_ONE**STEP
    corr_two = 1.0 - BETA_TWO**STEP

    def moments(k, ch):
        used = count > k
        rows = 64
        cols = slice(ch * tile, (ch + 1) * tile)

        @pl.loop(0, half // rows)
        def _(i):
            at = pl.ds(pl.multiple_of(i * rows, rows), rows)
            r = rot_own[at, :] + rot_recv[k, ch, at, :].astype(F32)
            m_old = one[at, k, cols]
            v_old = two[at, k, cols]
            m = BETA_ONE * m_old + (1.0 - BETA_ONE) * r
            v = BETA_TWO * v_old + (1.0 - BETA_TWO) * r * r
            one_new[at, k, cols] = jnp.where(used, m, m_old)
            two_new[at, k, cols] = jnp.where(used, v, v_old)
            normed[k, x, ch, at, :] = (
                m / corr_one / (jnp.sqrt(v / corr_two) + EPSILON)
            ).astype(BF)

        for d, s in enumerate(x_peers):
            go(
                normed.at[k, x, ch],
                normed.at[k, x, ch],
                ns_sem.at[k, d, ch],
                nr_sem.at[k, x, ch],
                {"sub": s},
            )

    def back_term(k, s, ch, n):
        return lax.dot_general(
            normed[k, s, ch],
            right[k, n * tile : (n + 1) * tile, columns(s, ch * tile)],
            (((1,), (1,)), ((), ())),
            preferred_element_type=F32,
        )

    def back_own(k):
        for n in range(chunks):
            total = back_term(k, x, 0, n)
            for ch in range(1, chunks):
                total = total + back_term(k, x, ch, n)
            back_sum[k, n] = total

    def back_rotate(k):
        for ch in range(chunks):
            for s in x_peers:
                arrive(normed.at[k, s, ch], nr_sem.at[k, s, ch], {"sub": s})
            for n in range(chunks):
                total = back_sum[k, n]
                for s in x_peers:
                    total = total + back_term(k, s, ch, n)
                if ch < chunks - 1:
                    back_sum[k, n] = total
                    continue
                back[k, n, c] = total.astype(BF)
                go(
                    back.at[k, n, c],
                    back.at[k, n, c],
                    bs_sem.at[k, n],
                    br_sem.at[k, n],
                    {"pair": 1 - c},
                )
        for n in range(chunks):
            arrive(back.at[k, n, 1 - c], br_sem.at[k, n], {"pair": 1 - c})
            step_send[k, n] = (
                jnp.dot(left[k], back[k, n].reshape(order, tile), preferred_element_type=F32)
                .astype(BF)
                .reshape(owners, shard, tile)
            )
            for d, o in enumerate(z_peers):
                go(
                    step_send.at[k, n, o],
                    step_recv.at[k, n, z],
                    us_sem.at[k, n, d],
                    ur_sem.at[k, n, z],
                    {"fsdp": o},
                )
            step_recv[k, n, z] = step_send[k, n, z]

    for k in range(last):
        rotate_right(k)
    loads[2].wait()
    loads[3].wait()
    for k in range(last):
        for ch in range(chunks):
            collect(k, ch)
            rotate_left(k, ch)
            moments(k, ch)
        back_own(k)
    rotate_right_last()
    for ch in range(chunks):
        rotate_left(last, ch)
        moments(last, ch)
    stores = [
        pltpu.make_async_copy(one_new, one_out, store_sem.at[0]),
        pltpu.make_async_copy(two_new, two_out, store_sem.at[1]),
    ]
    for store in stores:
        store.start()
    for k in range(last):
        back_rotate(k)
    back_own(last)
    back_rotate(last)
    for k in range(slots):
        for n in range(chunks):
            for p in z_peers:
                arrive(step_recv.at[k, n, p], ur_sem.at[k, n, p], {"fsdp": p})
    for n in range(chunks):
        for b in range(blocks):
            update[b, :, n * tile : (n + 1) * tile] = step_recv[
                jnp.minimum(rank[b], last), n, owner[b]
            ].astype(F32)
    for copy in pending:
        copy.wait_send()
    for store in stores:
        store.wait()


def shards(
    owners, subs, gradient, owner_table, left_basis, right_basis, first_moment, second_moment
):
    slots, order = right_basis.shape[1], right_basis.shape[3]
    blocks, shard, share = gradient.shape
    half = owners * shard
    left_rows = left_basis.reshape(slots, half, order)
    right_rows = right_basis.reshape(slots, share, order)
    one = first_moment.reshape(half, slots, share)
    two = second_moment.reshape(half, slots, share)
    tile = min(256, share)
    chunks = share // tile
    dma = pltpu.SemaphoreType.DMA
    whole = pl.BlockSpec(memory_space=pl.ANY)
    vmem = pl.BlockSpec(memory_space=pltpu.VMEM)
    moment = jax.ShapeDtypeStruct((half, slots, share), F32)
    update, new_one, new_two = pl.pallas_call(
        functools.partial(kernel, owners, subs),
        out_shape=(jax.ShapeDtypeStruct((blocks, shard, share), F32), moment, moment),
        in_specs=[pl.BlockSpec(memory_space=pltpu.SMEM), vmem, whole, whole, whole, whole],
        out_specs=(vmem, whole, whole),
        scratch_shapes=[
            pltpu.VMEM((slots, half, order), BF),
            pltpu.VMEM((slots, order, half), BF),
            pltpu.VMEM((slots, share, order), BF),
            pltpu.VMEM((half, slots, share), F32),
            pltpu.VMEM((half, slots, share), F32),
            pltpu.VMEM((half, slots, share), F32),
            pltpu.VMEM((half, slots, share), F32),
            pltpu.VMEM((blocks, shard, share), BF),
            pltpu.VMEM((subs, blocks, shard, share), BF),
            pltpu.VMEM((slots - 1, owners - 1, shard, share), BF),
            pltpu.VMEM((slots - 1, owners, shard, share), BF),
            pltpu.VMEM((subs, owners - 1, shard, share), BF),
            pltpu.VMEM((subs, owners, shard, share), BF),
            pltpu.VMEM((subs - 1, share // 2, share), BF),
            pltpu.VMEM((subs, 2, share // 2, share), BF),
            pltpu.VMEM((slots - 1, subs - 1, chunks, half, tile), BF),
            pltpu.VMEM((slots - 1, subs, chunks, half, tile), BF),
            pltpu.VMEM((slots, chunks, half, tile), BF),
            pltpu.VMEM((slots, chunks, half, tile), BF),
            pltpu.VMEM((slots, chunks, half, tile), BF),
            pltpu.VMEM((half, tile), F32),
            pltpu.VMEM((slots, subs, chunks, half, tile), BF),
            pltpu.VMEM((slots, chunks, half, tile), F32),
            pltpu.VMEM((slots, chunks, 2, half, tile), BF),
            pltpu.VMEM((slots, chunks, owners, shard, tile), BF),
            pltpu.VMEM((slots, chunks, owners, shard, tile), BF),
            dma((4,)),
            dma((2,)),
            dma((slots, owners)),
            dma((slots, owners)),
            dma((subs,)),
            dma((subs,)),
            dma((subs, owners)),
            dma((subs, owners)),
            dma((subs,)),
            dma((subs,)),
            dma((subs,)),
            dma((subs,)),
            dma((slots, subs, chunks)),
            dma((slots, subs, chunks)),
            dma((slots, chunks)),
            dma((slots, chunks)),
            dma((slots, subs, chunks)),
            dma((slots, subs, chunks)),
            dma((slots, chunks)),
            dma((slots, chunks)),
            dma((slots, chunks, owners)),
            dma((slots, chunks, owners)),
        ],
        compiler_params=pltpu.CompilerParams(
            collective_id=0, has_side_effects=True, vmem_limit_bytes=48 * 2**20
        ),
        cost_estimate=pl.CostEstimate(
            flops=10 * slots * half * order * share,
            bytes_accessed=20 * slots * half * share,
            transcendentals=slots * half * share,
        ),
    )(owner_table, gradient, left_rows, right_rows, one, two)
    return (update, new_one[None], new_two[None])


def solution(mesh):
    return jax.shard_map(
        functools.partial(shards, mesh.shape["fsdp"], mesh.shape["sub"]),
        mesh=mesh,
        in_specs=(
            P("groups", ("fsdp", "pair"), "sub"),
            P("groups"),
            P(("groups", "fsdp"), None, None, "pair", None, None),
            P(("groups", "fsdp"), None, "sub", None),
            P(("groups", "fsdp"), "pair", None, "sub"),
            P(("groups", "fsdp"), "pair", None, "sub"),
        ),
        out_specs=(
            P("groups", ("fsdp", "pair"), "sub"),
            P(("groups", "fsdp"), "pair", None, "sub"),
            P(("groups", "fsdp"), "pair", None, "sub"),
        ),
        check_vma=False,
    )
```

time: 87.1 us -> 80.1 us (0.920)
  the two profiles are of different devices: /device:TPU:29 before, /device:TPU:0 now
where the time goes in v2:
time: 80.1 us; the launch traced here: 79.9 us
  Pallas kernels  74 us (92%)
  local copies, waits for them, and re-layouts  5.3 us (7%)
    pallas_call x1, Pallas kernels, shards(): pl.pallas_call(functools.partial(kernel, owners, subs), out_shape=(jax.Sh...  74 us
    unnamed x7, local copies, waits for them, and re-layouts  5.3 us

profile of v2, /device:TPU:0, one launch (start us, length us, event | category | flops | bytes accessed | tf_op | source)
XLA Modules:
  0.0 79.9 jit_solution(11229786178388795211)
XLA Ops:
  0.6 0.0 copy-start
  0.6 1.1 %copy-done = f32[3,128,512]{2,1,0:T(8,128)S(1)} copy-done((f32[3,128,512]{2,1,0:T(8,128)S(1)}, f32[3,128,512]{2,1,0:T(8,128)}, u32[]{:S(2)}) %copy-start) | copy-done | bytes 786456
  1.8 0.0 copy-start.1
  1.8 0.7 copy-done.1
  2.4 74.0 %shard_map.85 = (f32[3,128,512]{2,1,0:T(8,128)S(1)}, f32[512,2,512]{2,1,0:T(2,128)S(1)}, f32[512,2,512]{2,1,0:T(2,128)S(1)}) custom-call(s32[3]{0:T(128)S(1)} %copy-done.1, f32[3,128,512]{2,1,0:T(8,128)S(1)} %copy-done, bf16[2,512,1024]{2,1,0:T(8,128)(2,1)} %bitcast.8, bf16[2,512,1024]{2,1,0:T(8,128)(2,1)} %bitcast.9, f32[512,2,512]{2,1,0:T(2,128)} %bitcast.10, ...), custom_call_target="tpu_custom_call" | custom-call | flops 5368709120 | bytes 10485760 | tf_op jit(solution)/shard_map/pallas_call | solution.py:404
  76.4 0.9 %copy.12 = f32[3,128,512]{2,1,0:T(8,128)} copy(f32[3,128,512]{2,1,0:T(8,128)S(1)} %get-tuple-element.12) | data formatting | bytes 1572864
  77.3 1.3 %copy.13 = f32[1,512,2,512]{3,2,1,0:T(2,128)} copy(f32[1,512,2,512]{3,2,1,0:T(2,128)S(1)} %bitcast.7) | data formatting | bytes 4194304
  78.6 1.3 %copy.14 = f32[1,512,2,512]{3,2,1,0:T(2,128)} copy(f32[1,512,2,512]{3,2,1,0:T(2,128)S(1)} %bitcast.6) | data formatting | bytes 4194304
Async XLA Ops:
  0.6 1.1 %copy-start = (f32[3,128,512]{2,1,0:T(8,128)S(1)}, f32[3,128,512]{2,1,0:T(8,128)}, u32[]{:S(2)}) copy-start(f32[3,128,512]{2,1,0:T(8,128)} %grad.1) | copy-start | bytes 2359300
  1.8 0.7 copy-start.1

commit v3 on v2

--- a/solution.py
+++ b/solution.py
@@ -76,6 +76,7 @@
     ar_sem,
     ls_sem,
     lr_sem,
+    cs_sem,
     fs_sem,
     fr_sem,
     hs_sem,
@@ -162,8 +163,50 @@
             copy.start()
             early.append(copy)
         grad_recv[k, z] = grad_own[source(z, k)]
-    for d, s in enumerate(x_peers):
-        go(grad_own, grad_far.at[x], as_sem.at[d], ar_sem.at[x], {"sub": s})
+    single = blocks < 2 * slots
+
+    def travel(t, way):
+        origin, after = z - way * t, z + way
+        here = (origin >= 0) & (origin < owners)
+        further = here & (after >= 0) & (after < owners)
+        return here, further, jnp.clip(origin, 0, owners - 1), jnp.clip(after, 0, owners - 1)
+
+    def chain(n, t, way, origin, after):
+        return send(
+            late_recv.at[n, origin],
+            late_recv.at[n, origin],
+            cs_sem.at[n, t, (1 - way) // 2],
+            lr_sem.at[n, origin],
+            {"fsdp": after},
+        )
+
+    def hop(n, t):
+        for way in (1, -1):
+            here, further, origin, after = travel(t, way)
+            if t > 0:
+
+                @pl.when(here)
+                def _():
+                    arrive(late_recv.at[n, origin], lr_sem.at[n, origin], {"fsdp": origin})
+
+            if t < owners - 1:
+
+                @pl.when(further)
+                def _():
+                    chain(n, t, way, origin, after).start()
+
+    if single:
+        only = jnp.int32(0)
+        for b in range(blocks):
+            only = only + jnp.where(rank[b] == last, b, 0)
+        late_recv[0, z] = grad_own[jnp.minimum(only, blocks - 1)]
+        for d, s in enumerate(x_peers):
+            n = subs - 1 - d
+            go(late_recv.at[0, z], late_recv.at[n, z], as_sem.at[d], ar_sem.at[n], {"sub": s})
+        hop(0, 0)
+    else:
+        for d, s in enumerate(x_peers):
+            go(grad_own, grad_far.at[x], as_sem.at[d], ar_sem.at[x], {"sub": s})
 
     def columns(s, n):
         return pl.ds(pl.multiple_of(s * share + n, tile), tile)
@@ -181,26 +224,32 @@
         for n in range(0, half, tile):
             left_t[k, :, n : n + tile] = left[k, n : n + tile, :].T
 
-    for copy in early:
-        copy.wait_send()
-    for n, s in enumerate([x] + x_peers):
-        if n == 1:
-            for p in x_peers:
-                arrive(grad_far.at[p], ar_sem.at[p], {"sub": p})
-        rows = (lambda i: grad_far[s, i]) if n else (lambda i: grad_own[i])
-        for d, o in enumerate(z_peers):
-            late_send[n, d] = rows(source(o, last))
-            go(
-                late_send.at[n, d],
-                late_recv.at[n, z],
-                ls_sem.at[n, d],
-                lr_sem.at[n, z],
-                {"fsdp": o},
-            )
-        late_recv[n, z] = rows(source(z, last))
+    if single:
+        for n in range(1, subs):
+            arrive(late_recv.at[n, z], ar_sem.at[n], {"sub": x_peers[n - 1]})
+            hop(n, 0)
+    else:
+        for n, s in enumerate([x] + x_peers):
+            if n == 1:
+                for p in x_peers:
+                    arrive(grad_far.at[p], ar_sem.at[p], {"sub": p})
+            rows = (lambda i: grad_far[s, i]) if n else (lambda i: grad_own[i])
+            for d, o in enumerate(z_peers):
+                late_send[n, d] = rows(source(o, last))
+                go(
+                    late_send.at[n, d],
+                    late_recv.at[n, z],
+                    ls_sem.at[n, d],
+                    lr_sem.at[n, z],
+                    {"fsdp": o},
+                )
+            late_recv[n, z] = rows(source(z, last))
     for d, s in enumerate(x_peers):
         arrive(far.at[s, c], fr_sem.at[s], {"sub": s})
         go(far.at[s, c], far.at[s, c], hs_sem.at[d], hr_sem.at[d], {"pair": 1 - c})
+    if single and owners > 2:
+        for n in range(subs):
+            hop(n, 1)
 
     def rotate_right(k):
         for p in z_peers:
@@ -232,6 +281,9 @@
 
     def rotate_right_last():
         for n in range(subs):
+            if single:
+                hop(n, owners - 1)
+                continue
             for p in z_peers:
                 arrive(late_recv.at[n, p], lr_sem.at[n, p], {"fsdp": p})
         for d, s in enumerate(x_peers):
@@ -348,6 +400,10 @@
 
     for k in range(last):
         rotate_right(k)
+    if single:
+        for t in range(2, owners - 1):
+            for n in range(subs):
+                hop(n, t)
     loads[2].wait()
     loads[3].wait()
     for k in range(last):
@@ -379,8 +435,18 @@
             update[b, :, n * tile : (n + 1) * tile] = step_recv[
                 jnp.minimum(rank[b], last), n, owner[b]
             ].astype(F32)
-    for copy in pending:
+    for copy in early + pending:
         copy.wait_send()
+    if single:
+        for n in range(subs):
+            for t in range(owners - 1):
+                for way in (1, -1):
+                    _, further, origin, after = travel(t, way)
+
+                    @pl.when(further)
+                    def _():
+                        chain(n, t, way, origin, after).wait_send()
+
     for store in stores:
         store.wait()
 
@@ -441,6 +507,7 @@
             dma((subs,)),
             dma((subs, owners)),
             dma((subs, owners)),
+            dma((subs, owners, 2)),
             dma((subs,)),
             dma((subs,)),
             dma((subs,)),

time: 80.1 us -> 80.4 us (level)
  no operation moved by 1% of the time
where the time goes in v3:
time: 80.4 us; the launch traced here: 80.3 us
  Pallas kernels  74.3 us (92%)
  local copies, waits for them, and re-layouts  5.3 us (7%)
    pallas_call x1, Pallas kernels, shards(): pl.pallas_call(functools.partial(kernel, owners, subs), out_shape=(jax.Sh...  74.3 us
    unnamed x7, local copies, waits for them, and re-layouts  5.3 us

profile of v3, /device:TPU:0, one launch (start us, length us, event | category | flops | bytes accessed | tf_op | source)
XLA Modules:
  0.0 80.3 jit_solution(273481680105511093)
XLA Ops:
  0.6 0.0 copy-start
  0.6 1.1 %copy-done = f32[3,128,512]{2,1,0:T(8,128)S(1)} copy-done((f32[3,128,512]{2,1,0:T(8,128)S(1)}, f32[3,128,512]{2,1,0:T(8,128)}, u32[]{:S(2)}) %copy-start) | copy-done | bytes 786456
  1.8 0.0 copy-start.1
  1.8 0.7 copy-done.1
  2.4 74.3 %shard_map.85 = (f32[3,128,512]{2,1,0:T(8,128)S(1)}, f32[512,2,512]{2,1,0:T(2,128)S(1)}, f32[512,2,512]{2,1,0:T(2,128)S(1)}) custom-call(s32[3]{0:T(128)S(1)} %copy-done.1, f32[3,128,512]{2,1,0:T(8,128)S(1)} %copy-done, bf16[2,512,1024]{2,1,0:T(8,128)(2,1)} %bitcast.8, bf16[2,512,1024]{2,1,0:T(8,128)(2,1)} %bitcast.9, f32[512,2,512]{2,1,0:T(2,128)} %bitcast.10, ...), custom_call_target="tpu_custom_call" | custom-call | flops 5368709120 | bytes 10485760 | tf_op jit(solution)/shard_map/pallas_call | solution.py:470
  76.8 0.9 %copy.12 = f32[3,128,512]{2,1,0:T(8,128)} copy(f32[3,128,512]{2,1,0:T(8,128)S(1)} %get-tuple-element.12) | data formatting | bytes 1572864
  77.6 1.3 %copy.13 = f32[1,512,2,512]{3,2,1,0:T(2,128)} copy(f32[1,512,2,512]{3,2,1,0:T(2,128)S(1)} %bitcast.7) | data formatting | bytes 4194304
  79.0 1.3 %copy.14 = f32[1,512,2,512]{3,2,1,0:T(2,128)} copy(f32[1,512,2,512]{3,2,1,0:T(2,128)S(1)} %bitcast.6) | data formatting | bytes 4194304
Async XLA Ops:
  0.6 1.1 %copy-start = (f32[3,128,512]{2,1,0:T(8,128)S(1)}, f32[3,128,512]{2,1,0:T(8,128)}, u32[]{:S(2)}) copy-start(f32[3,128,512]{2,1,0:T(8,128)} %grad.1) | copy-start | bytes 2359300
  1.8 0.7 copy-start.1

commit v4 on v3

--- a/solution.py
+++ b/solution.py
@@ -247,9 +247,6 @@
     for d, s in enumerate(x_peers):
         arrive(far.at[s, c], fr_sem.at[s], {"sub": s})
         go(far.at[s, c], far.at[s, c], hs_sem.at[d], hr_sem.at[d], {"pair": 1 - c})
-    if single and owners > 2:
-        for n in range(subs):
-            hop(n, 1)
 
     def rotate_right(k):
         for p in z_peers:
@@ -335,7 +332,7 @@
             one_new[at, k, cols] = jnp.where(used, m, m_old)
             two_new[at, k, cols] = jnp.where(used, v, v_old)
             normed[k, x, ch, at, :] = (
-                m / corr_one / (jnp.sqrt(v / corr_two) + EPSILON)
+                m * (1.0 / corr_one) / (jnp.sqrt(v * (1.0 / corr_two)) + EPSILON)
             ).astype(BF)
 
         for d, s in enumerate(x_peers):
@@ -400,10 +397,9 @@
 
     for k in range(last):
         rotate_right(k)
-    if single:
-        for t in range(2, owners - 1):
-            for n in range(subs):
-                hop(n, t)
+    if single and owners > 2:
+        for n in range(subs):
+            hop(n, 1)
     loads[2].wait()
     loads[3].wait()
     for k in range(last):
@@ -411,7 +407,10 @@
             collect(k, ch)
             rotate_left(k, ch)
             moments(k, ch)
-        back_own(k)
+            if single and k == 0 and ch == 0:
+                for t in range(2, owners - 1):
+                    for n in range(subs):
+                        hop(n, t)
     rotate_right_last()
     for ch in range(chunks):
         rotate_left(last, ch)
@@ -423,6 +422,7 @@
     for store in stores:
         store.start()
     for k in range(last):
+        back_own(k)
         back_rotate(k)
     back_own(last)
     back_rotate(last)

time: 80.4 us -> 74.9 us (0.932)
  Pallas kernels: 74.3 us -> 68.7 us
    pallas_call x1, Pallas kernels: 74.3 us -> 68.7 us  [shards(): pl.pallas_call(functools.partial(kernel, owners, subs), out_shape=(jax.Sh...]
where the time goes in v4:
time: 74.9 us; the launch traced here: 74.7 us
  Pallas kernels  68.7 us (92%)
  local copies, waits for them, and re-layouts  5.3 us (7%)
    pallas_call x1, Pallas kernels, shards(): pl.pallas_call(functools.partial(kernel, owners, subs), out_shape=(jax.Sh...  68.7 us
    unnamed x7, local copies, waits for them, and re-layouts  5.3 us

profile of v4, /device:TPU:0, one launch (start us, length us, event | category | flops | bytes accessed | tf_op | source)
XLA Modules:
  0.0 74.7 jit_solution(15007481758230468838)
XLA Ops:
  0.6 0.0 copy-start
  0.6 1.1 %copy-done = f32[3,128,512]{2,1,0:T(8,128)S(1)} copy-done((f32[3,128,512]{2,1,0:T(8,128)S(1)}, f32[3,128,512]{2,1,0:T(8,128)}, u32[]{:S(2)}) %copy-start) | copy-done | bytes 786456
  1.8 0.0 copy-start.1
  1.8 0.7 copy-done.1
  2.4 68.7 %shard_map.85 = (f32[3,128,512]{2,1,0:T(8,128)S(1)}, f32[512,2,512]{2,1,0:T(2,128)S(1)}, f32[512,2,512]{2,1,0:T(2,128)S(1)}) custom-call(s32[3]{0:T(128)S(1)} %copy-done.1, f32[3,128,512]{2,1,0:T(8,128)S(1)} %copy-done, bf16[2,512,1024]{2,1,0:T(8,128)(2,1)} %bitcast.8, bf16[2,512,1024]{2,1,0:T(8,128)(2,1)} %bitcast.9, f32[512,2,512]{2,1,0:T(2,128)} %bitcast.10, ...), custom_call_target="tpu_custom_call" | custom-call | flops 5368709120 | bytes 10485760 | tf_op jit(solution)/shard_map/pallas_call | solution.py:470
  71.2 0.9 %copy.12 = f32[3,128,512]{2,1,0:T(8,128)} copy(f32[3,128,512]{2,1,0:T(8,128)S(1)} %get-tuple-element.12) | data formatting | bytes 1572864
  72.1 1.3 %copy.13 = f32[1,512,2,512]{3,2,1,0:T(2,128)} copy(f32[1,512,2,512]{3,2,1,0:T(2,128)S(1)} %bitcast.7) | data formatting | bytes 4194304
  73.4 1.3 %copy.14 = f32[1,512,2,512]{3,2,1,0:T(2,128)} copy(f32[1,512,2,512]{3,2,1,0:T(2,128)S(1)} %bitcast.6) | data formatting | bytes 4194304
Async XLA Ops:
  0.6 1.1 %copy-start = (f32[3,128,512]{2,1,0:T(8,128)S(1)}, f32[3,128,512]{2,1,0:T(8,128)}, u32[]{:S(2)}) copy-start(f32[3,128,512]{2,1,0:T(8,128)} %grad.1) | copy-start | bytes 2359300
  1.8 0.7 copy-start.1
